TPU v7x, 32 devices: a whole 2x2x4 slice. The times are simulated.
32 devices in a mesh: space: 8 (over z, x), segment: 4 (over y, core).
Axes of the slice: x: 2, y: 2, z: 4, core: 2. Of those that a mesh axis runs over, the one named last changes fastest.
Arguments:
- field: bfloat16 [4, 64, 8, 8, 128], P(None, 'space'), may hold values from -6 to 6
- depth_kernel: bfloat16 [8, 49, 128], P('segment'), may hold values from -0.875 to 0.875
- depth_bias: bfloat16 [8, 128], P('segment'), may hold values from -3 to 3
- norm_gain: bfloat16 [8, 128], P('segment'), may hold values from 0.099609375 to 1.8984375
- up_weight: bfloat16 [8, 128, 512], P('segment'), may hold values from -0.5 to 0.5
- up_bias: bfloat16 [8, 512], P('segment'), may hold values from -3 to 3
- down_weight: bfloat16 [8, 512, 128], P('segment'), may hold values from -0.25 to 0.25
- scale_exponent: int32 [8, 128], P('segment'), may hold values from -3 to 1
- live_count: int32 [8], P('space'), may hold values from 4 to 8, as said below
- neighbours: int32 [64, 8], P('space'), may hold values from -1 to 63, as said below
- rotations: int32 [64, 8], P('space'), may hold values from 0 to 3
Outputs:
- boundary: bfloat16 [4, 4, 64, 8, 8, 128], P('segment', None, 'space')
Inputs may be any that keep to these rules, and one draw needn't show every extreme that they name: `live_count`: at least one index of space holds 8 land patches. `neighbours`: every entry of a live slot is -1, a live slot of the same index of space, one of the first 1 slots of the next index along space, or one of the last 1 slots of the previous one, counted around the cycle; entries of slots that are not live are -1.
All inputs are finite; a program needn't handle non-finite values.
Results may differ from a plain program's by a relative error of at most 0.03.
Values may be sent and summed in bfloat16 or wider, within the bound.
A program may use at most 64 MiB of HBM per device.

v0:
```python
import functools

import jax
import jax.numpy as jnp
import numpy as np
from jax import lax
from jax.experimental import pallas as pl
from jax.experimental.pallas import tpu as pltpu
from jax.sharding import PartitionSpec as P

KS = 7
BPS = 2
EDGE = 1
MARGIN = KS // 2
PS = 8
CELLS = PS * PS
EXT = PS + 2 * MARGIN
PITCH = 15
ROWS = 224
LANES = 256
MESH = pl.DeviceIdType.MESH

BIAS = KS * KS
GAIN = BIAS + 1
SCALE = GAIN + 1
UP_BIAS = SCALE + 1


def tables():
    table = np.zeros((8, LANES), np.int32)
    table[0] = -1
    last = PS - 1
    for j in range(EXT):
        for i in range(EXT):
            band_i = 0 if i < MARGIN else (1 if i < MARGIN + PS else 2)
            band_j = 0 if j < MARGIN else (1 if j < MARGIN + PS else 2)
            u = (i + PS - MARGIN) % PS
            v = (j + PS - MARGIN) % PS
            r = j * PITCH + i
            table[0, r] = ((0, 1, 2), (3, 8, 4), (5, 6, 7))[band_i][band_j]
            turned = ((u, v), (v, last - u), (last - u, last - v), (last - v, u))
            for k, (p, q) in enumerate(turned):
                table[1 + k, r] = p * PS + q
    return table


def targets(neighbours, rotations, table, place, devices):
    count = neighbours.shape[0]
    local = neighbours - place * count
    following = lax.rem(place + 1, devices) * count
    slot = jnp.where(neighbours == following, count + 1, count)
    slot = jnp.where(jnp.logical_and(local >= 0, local < count), local, slot)
    slot = jnp.where(neighbours < 0, -1, slot)
    shape = (count, LANES)
    link = jnp.full(shape, -1, jnp.int32)
    turn = jnp.zeros(shape, jnp.int32)
    direction = jnp.broadcast_to(table[0:1, :], shape)
    for d in range(8):
        here = direction == d
        link = jnp.where(here, jnp.broadcast_to(slot[:, d : d + 1], shape), link)
        turn = jnp.where(here, jnp.broadcast_to(rotations[:, d : d + 1], shape), turn)
    link = jnp.where(direction == 8, lax.broadcasted_iota(jnp.int32, shape, 0), link)
    cell = jnp.broadcast_to(table[1:2, :], shape)
    for k in range(1, 4):
        cell = jnp.where(turn == k, jnp.broadcast_to(table[1 + k : 2 + k, :], shape), cell)
    return jnp.where(link < 0, -1, link * CELLS + cell)


def gelu(x):
    return 0.5 * x * (1.0 + lax.erf(x * np.float32(0.5**0.5)))


def kernel(
    segments,
    devices,
    blocks,
    field,
    taps,
    bias,
    gain,
    up,
    up_bias,
    down,
    scale,
    live_count,
    neighbours,
    rotations,
    table,
    out,
    v_taps,
    v_bias,
    v_gain,
    v_up_bias,
    v_scale,
    v_neighbours,
    v_rotations,
    v_table,
    win,
    ups,
    downs,
    small,
    route,
    ext,
    loc_sem,
    own_sem,
    w_recv,
    fwd_sem,
    h_send,
    h_recv,
    o_send,
    o_recv,
    in_sem,
):
    space = lax.axis_index("space")
    me = lax.axis_index("segment")
    count = win.shape[1] // CELLS - 2
    rows = count * CELLS
    after = lax.rem(space + 1, devices)
    before = lax.rem(space + devices - 1, devices)
    core = lax.rem(me, 2)
    pair = me // 2
    partner = pair * 2 + (1 - core)
    pairs = segments // 2
    mine = me * BPS

    start_field = pltpu.make_async_copy(field.at[me], win.at[0, pl.ds(0, rows)], loc_sem.at[0])
    start_field.start()
    own_up = pltpu.make_async_copy(up, ups.at[pl.ds(mine, BPS)], loc_sem.at[1])
    own_up.start()
    own_down = pltpu.make_async_copy(down, downs.at[pl.ds(mine, BPS)], loc_sem.at[2])
    own_down.start()
    loads = [
        pltpu.make_async_copy(src, dst, in_sem.at[n])
        for n, (src, dst) in enumerate(
            (
                (taps, v_taps),
                (bias, v_bias),
                (gain, v_gain),
                (up_bias, v_up_bias),
                (scale, v_scale),
                (neighbours, v_neighbours),
                (rotations, v_rotations),
                (table, v_table),
            )
        )
    ]
    for load in loads:
        load.start()
    order = [count - 1, *range(count - 1)]
    half = 2 + (count - 2) // 2
    hid = up_bias.shape[1]
    chans = up.shape[1]
    barrier = pltpu.get_barrier_semaphore()
    for step in range(1, segments):
        pl.semaphore_signal(
            barrier,
            inc=1,
            device_id=(space, lax.rem(me + step, segments)),
            device_id_type=MESH,
        )
    for side in (before, after):
        pl.semaphore_signal(barrier, inc=1, device_id=(side, me), device_id_type=MESH)

    for load in loads:
        load.wait()
    for k in range(BPS):
        small[mine + k, 0 : KS * KS, :] = v_taps[:, k, :].astype(jnp.float32)
        small[mine + k, BIAS : BIAS + 1, :] = v_bias[k : k + 1, :].astype(jnp.float32)
        small[mine + k, GAIN : GAIN + 1, :] = v_gain[k : k + 1, :].astype(jnp.float32)
        small[mine + k, SCALE : SCALE + 1, :] = jnp.exp2(
            v_scale[k : k + 1, :].astype(jnp.float32) * 0.5
        )
        for q in range(hid // chans):
            small[mine + k, UP_BIAS + q : UP_BIAS + q + 1, :] = v_up_bias[
                k : k + 1, q * chans : (q + 1) * chans
            ].astype(jnp.float32)
    pl.semaphore_wait(barrier, segments + 1)

    def halo(b, side):
        if side == 0:
            src = win.at[b, pl.ds(rows - CELLS, CELLS)]
            dst, to = win.at[b, pl.ds(rows, CELLS)], after
        else:
            src = win.at[b, pl.ds(0, CELLS)]
            dst, to = win.at[b, pl.ds(rows + CELLS, CELLS)], before
        return pltpu.make_async_remote_copy(
            src_ref=src,
            dst_ref=dst,
            send_sem=h_send.at[b, side],
            recv_sem=h_recv.at[b, side],
            device_id=(to, me),
            device_id_type=MESH,
        )

    def piece(kind, b, to, send_sem):
        ref = (small, ups, downs)[kind].at[b]
        return pltpu.make_async_remote_copy(
            src_ref=ref,
            dst_ref=ref,
            send_sem=send_sem,
            recv_sem=w_recv.at[kind, b],
            device_id=(space, to),
            device_id_type=MESH,
        )

    def to_partner():
        return [
            piece(kind, mine + k, partner, own_sem.at[k, kind])
            for k in range(BPS)
            for kind in range(3)
        ]

    def to_pairs(k):
        copies = []
        for step in range(1, pairs):
            other = lax.rem(pair + step, pairs) * 2
            at = 3 + (step - 1) * 4
            copies.append(piece(0, mine + k, other, own_sem.at[k, at]))
            copies.append(piece(0, mine + k, other + 1, own_sem.at[k, at + 1]))
            copies.append(piece(1, mine + k, other, own_sem.at[k, at + 2]))
            copies.append(piece(2, mine + k, other + 1, own_sem.at[k, at + 3]))
        return copies

    def forwarded(b, act):
        foreign = b // (2 * BPS) != pair

        @pl.when(jnp.logical_and(foreign, core == 0))
        def _():
            act(piece(1, b, partner, fwd_sem.at[b]))

        @pl.when(jnp.logical_and(foreign, core == 1))
        def _():
            act(piece(2, b, partner, fwd_sem.at[b]))

    def forward(b):
        def act(copy):
            copy.wait_recv()
            copy.start()

        forwarded(b, act)

    def arrive(b):
        owner = b // BPS
        foreign = b // (2 * BPS) != pair

        @pl.when(owner != me)
        def _():
            piece(0, b, partner, fwd_sem.at[b]).wait_recv()

        @pl.when(owner == partner)
        def _():
            piece(1, b, partner, fwd_sem.at[b]).wait_recv()
            piece(2, b, partner, fwd_sem.at[b]).wait_recv()

        @pl.when(jnp.logical_and(foreign, core == 0))
        def _():
            piece(2, b, partner, fwd_sem.at[b]).wait_recv()

        @pl.when(jnp.logical_and(foreign, core == 1))
        def _():
            piece(1, b, partner, fwd_sem.at[b]).wait_recv()

    def result(s):
        return win.at[BPS * (s + 1), pl.ds(0, rows)]

    def send_result(s):
        return pltpu.make_async_remote_copy(
            src_ref=result(s),
            dst_ref=out.at[me],
            send_sem=o_send.at[s],
            recv_sem=o_recv.at[me],
            device_id=(space, s),
            device_id_type=MESH,
        )

    def keep_result(s):
        return pltpu.make_async_copy(result(s), out.at[me], loc_sem.at[3])

    def build_route():
        target = targets(
            v_neighbours[...], v_rotations[...], v_table[...], space, devices
        )
        target = jnp.transpose(target.astype(jnp.float32))
        columns = lax.broadcasted_iota(jnp.int32, (ROWS, win.shape[1]), 1).astype(jnp.float32)
        for g in range(count):
            hit = jnp.broadcast_to(target[0:ROWS, g : g + 1], columns.shape) == columns
            at = order.index(g) * ROWS
            route[at : at + ROWS, :] = jnp.where(hit, 1.0, 0.0).astype(jnp.bfloat16)

    def gather(b, first, last):
        ext[first * ROWS : last * ROWS, :] = jnp.dot(
            route[first * ROWS : last * ROWS, :], win[b], preferred_element_type=jnp.float32
        )

    def convolve(b, n):
        total = jnp.broadcast_to(small[b, BIAS : BIAS + 1, :][None], (PS, PS, chans))
        for e in range(KS):
            base = n * ROWS + e * PITCH
            column = jnp.concatenate(
                [ext[pl.ds(base + i, PS, stride=PITCH), :][None] for i in range(EXT)], axis=0
            )
            for a in range(KS):
                tap = small[b, a * KS + e : a * KS + e + 1, :][None]
                total = total + column[a : a + PS] * tap
        total = total.reshape(CELLS, chans)
        centred = total - jnp.mean(total, axis=-1, keepdims=True)
        variance = jnp.mean(centred * centred, axis=-1, keepdims=True)
        scaled = centred * lax.rsqrt(variance + 1e-06) * small[b, GAIN : GAIN + 1, :]
        return scaled.astype(jnp.bfloat16)

    def group(b, first, last):
        normed = jnp.concatenate([convolve(b, n) for n in range(first, last)], axis=0)
        wide = jnp.concatenate(
            [small[b, UP_BIAS + q : UP_BIAS + q + 1, :] for q in range(hid // chans)], axis=1
        )
        hidden = jnp.dot(normed, ups[b], preferred_element_type=jnp.float32) + wide
        hidden = gelu(hidden).astype(jnp.bfloat16)
        branch = jnp.dot(hidden, downs[b], preferred_element_type=jnp.float32)
        branch = branch * small[b, SCALE : SCALE + 1, :]
        for n in range(first, last):
            g = order[n]
            at = pl.ds(g * CELLS, CELLS)
            alive = jnp.logical_or(g < live_count[0] - EDGE, g >= count - EDGE)
            here = branch[(n - first) * CELLS : (n - first + 1) * CELLS]
            state = win[b, at, :].astype(jnp.float32) + here
            win[b + 1, at, :] = (state * jnp.where(alive, 1.0, 0.0)).astype(jnp.bfloat16)

    start_field.wait()
    halo(0, 0).start()
    halo(0, 1).start()
    own_up.wait()
    own_down.wait()

    @pl.when(core == 0)
    def _():
        for copy in to_pairs(0):
            copy.start()

    for copy in to_partner():
        copy.start()
    build_route()
    forward(0)

    def layer(b, carry, final=False):
        arrive(b)
        for k in range(BPS):
            for c in range(2):
                if k + c:

                    @pl.when(jnp.logical_and(b == k + 2 * c - 1, core == c))
                    def _():
                        for copy in to_pairs(k):
                            copy.start()

        halo(b, 0).wait_recv()
        halo(b, 1).wait_recv()
        gather(b, 0, 2)
        group(b, 0, 2)
        if not final:
            halo(b + 1, 0).start()
            halo(b + 1, 1).start()
        gather(b, 2, count)
        group(b, 2, half)
        if not final:
            forward(b + 1)
        group(b, half, count)
        s = b // BPS
        ends = lax.rem(b, BPS) == BPS - 1

        @pl.when(jnp.logical_and(ends, s != me))
        def _():
            send_result(s).start()

        @pl.when(jnp.logical_and(ends, s == me))
        def _():
            keep_result(s).start()

        return carry

    lax.fori_loop(0, blocks - 1, layer, 0)
    layer(blocks - 1, 0, final=True)

    for copy in to_partner() + [copy for k in range(BPS) for copy in to_pairs(k)]:
        copy.wait_send()

    def drain(b, carry):
        halo(b, 0).wait_send()
        halo(b, 1).wait_send()
        forwarded(b, lambda copy: copy.wait_send())
        return carry

    lax.fori_loop(0, blocks, drain, 0)
    keep_result(me).wait()
    for step in range(1, segments):
        send_result(lax.rem(me + step, segments)).wait_send()
    for step in range(1, segments):
        other = lax.rem(me + step, segments)
        pltpu.make_async_remote_copy(
            src_ref=result(0),
            dst_ref=out.at[other],
            send_sem=o_send.at[other],
            recv_sem=o_recv.at[other],
            device_id=(space, other),
            device_id_type=MESH,
        ).wait_recv()


def body(
    field,
    depth_kernel,
    depth_bias,
    norm_gain,
    up_weight,
    up_bias,
    down_weight,
    scale_exponent,
    live_count,
    neighbours,
    rotations,
):
    members, count = field.shape[:2]
    chans = field.shape[-1]
    hid = up_weight.shape[-1]
    segments = lax.axis_size("segment")
    devices = lax.axis_size("space")
    blocks = segments * BPS
    assert members == segments and segments % 2 == 0 and count % 2 == 0
    pairs = segments // 2
    smalls = -(-(UP_BIAS + hid // chans) // 8) * 8
    smem = pl.BlockSpec(memory_space=pltpu.SMEM)
    hbm = pl.BlockSpec(memory_space=pl.ANY)
    dma = pltpu.SemaphoreType.DMA
    out = pl.pallas_call(
        functools.partial(kernel, segments, devices, blocks),
        out_shape=jax.ShapeDtypeStruct((members, count * CELLS, chans), jnp.bfloat16),
        in_specs=[hbm] * 8 + [smem] + [hbm] * 3,
        out_specs=pl.BlockSpec(memory_space=pl.ANY),
        scratch_shapes=[
            pltpu.VMEM((KS * KS, BPS, chans), jnp.bfloat16),
            pltpu.VMEM((BPS, chans), jnp.bfloat16),
            pltpu.VMEM((BPS, chans), jnp.bfloat16),
            pltpu.VMEM((BPS, hid), jnp.bfloat16),
            pltpu.VMEM((BPS, chans), jnp.int32),
            pltpu.VMEM(neighbours.shape, jnp.int32),
            pltpu.VMEM(rotations.shape, jnp.int32),
            pltpu.VMEM((8, LANES), jnp.int32),
            pltpu.VMEM((blocks + 1, (count + 2) * CELLS, chans), jnp.bfloat16),
            pltpu.VMEM((blocks, chans, hid), jnp.bfloat16),
            pltpu.VMEM((blocks, hid, chans), jnp.bfloat16),
            pltpu.VMEM((blocks, smalls, chans), jnp.float32),
            pltpu.VMEM((count * ROWS, (count + 2) * CELLS), jnp.bfloat16),
            pltpu.VMEM((count * ROWS, chans), jnp.float32),
            dma((4,)),
            dma((BPS, 3 + 4 * (pairs - 1))),
            dma((3, blocks)),
            dma((blocks,)),
            dma((blocks, 2)),
            dma((blocks, 2)),
            dma((segments,)),
            dma((members,)),
            dma((8,)),
        ],
        compiler_params=pltpu.CompilerParams(
            collective_id=0, has_side_effects=True, vmem_limit_bytes=60 * 2**20
        ),
    )(
        field.reshape(members, count * CELLS, chans),
        jnp.transpose(depth_kernel, (1, 0, 2)),
        depth_bias,
        norm_gain,
        up_weight,
        up_bias,
        down_weight,
        scale_exponent,
        live_count,
        neighbours,
        rotations,
        jnp.asarray(tables()),
    )
    return out.reshape((1,) + field.shape)


def solution(mesh):
    in_specs = (
        P(None, "space", None, None, None),
        P("segment", None, None),
        P("segment", None),
        P("segment", None),
        P("segment", None, None),
        P("segment", None),
        P("segment", None, None),
        P("segment", None),
        P("space"),
        P("space", None),
        P("space", None),
    )
    out_specs = P("segment", None, "space", None, None, None)
    return jax.shard_map(body, mesh=mesh, in_specs=in_specs, out_specs=out_specs, check_vma=False)
```

profile of v0, /device:TPU:0, one launch (start us, length us, event | category | flops | bytes accessed | tf_op | source)
XLA Modules:
  0.0 55.4 jit_solution(14931802885770807574)
XLA Ops:
  0.7 52.8 %shard_map.118 = bf16[4,512,128]{2,1,0:T(8,128)(2,1)} custom-call(bf16[4,512,128]{2,1,0:T(8,128)(2,1)} %bitcast.4, bf16[49,2,128]{2,1,0:T(2,128)(2,1)} %bitcast.5, bf16[2,128]{1,0:T(2,128)(2,1)} %bias.1, bf16[2,128]{1,0:T(2,128)(2,1)} %gain.1, bf16[2,128,512]{2,1,0:T(8,128)(2,1)} %up.1, bf16[2,512]{1,0:T(2,128)(2,1)} %up_bias.1, bf16[2,512,128]{2,1,0:T(8,128)(2,1)} %down.1, ...), custom_call_target="tpu_custom_call" | custom-call | tf_op jit(solution)/shard_map/pallas_call | solution.py:433
  53.5 1.9 %copy.15 = bf16[1,4,8,8,8,128]{5,4,3,2,1,0:T(8,128)(2,1)} copy(bf16[1,4,8,8,8,128]{5,4,3,2,1,0:T(8,128)(2,1)} %bitcast.3) | data formatting | bytes 1048576
where the time goes:
time: 55.6 us; the launch traced here: 55.4 us
  Pallas kernels  52.8 us (95%)
  local copies, waits for them, and re-layouts  1.87 us (3%)
  between operations  0.66 us (1%)
    pallas_call x1, Pallas kernels, body(): pl.pallas_call(functools.partial(kernel, segments, devices, blocks), out_...  52.8 us
    unnamed x1, local copies, waits for them, and re-layouts  1.87 us

commit v1 on v0

v1 whole, which is shorter than its diff:
```python
import functools

import jax
import jax.numpy as jnp
import numpy as np
from jax import lax
from jax.experimental import pallas as pl
from jax.experimental.pallas import tpu as pltpu
from jax.sharding import PartitionSpec as P

KS = 7
BPS = 2
EDGE = 1
MARGIN = KS // 2
PS = 8
CELLS = PS * PS
EXT = PS + 2 * MARGIN
WIDE = 3 * PS
ROWS = EXT * WIDE
TURNS = 4
MESH = pl.DeviceIdType.MESH
HOLDERS = {8: (0, 1, 2, 3, 5, 7, 6, 4)}

BIAS = KS * KS
GAIN = BIAS + 1
SCALE = GAIN + 1
UP_BIAS = SCALE + 1


def bases(neighbours, rotations, place, devices, tiles):
    count = neighbours.shape[0]
    local = neighbours - place * count
    following = lax.rem(place + 1, devices) * count
    slot = jnp.where(neighbours == following, count + 1, count)
    slot = jnp.where(jnp.logical_and(local >= 0, local < count), local, slot)
    slot = jnp.where(neighbours < 0, count + 2, slot)
    return (rotations * tiles + slot) * PS


def lookup(table, index):
    value = index
    for k, entry in enumerate(table):
        if entry != k:
            value = jnp.where(index == k, entry, value)
    return value


def position(space, devices):
    return lookup([HOLDERS.get(devices, range(devices)).index(k) for k in range(devices)], space)


def holder(place, devices):
    return lookup(HOLDERS.get(devices, range(devices)), place)


def gelu2(x):
    return x * (1.0 + lax.erf(x * np.float32(0.5**0.5)))


def kernel(
    segments,
    devices,
    blocks,
    field,
    taps,
    bias,
    gain,
    up,
    up_bias,
    down,
    scale,
    live_count,
    neighbours,
    rotations,
    out,
    v_taps,
    v_bias,
    v_gain,
    v_up_bias,
    v_scale,
    v_neighbours,
    v_rotations,
    meta,
    here,
    links,
    win,
    edges,
    ups,
    downs,
    small,
    tiles_a,
    tiles_b,
    ext,
    loc_sem,
    own_sem,
    w_recv,
    fwd_sem,
    h_send,
    h_recv,
    f_send,
    f_recv,
    o_send,
    o_recv,
    in_sem,
):
    space = lax.axis_index("space")
    me = lax.axis_index("segment")
    rows = win.shape[1]
    count = rows // CELLS
    tiles = count + 3
    place = position(space, devices)
    following = lax.rem(place + 1, devices)
    preceding = lax.rem(place + devices - 1, devices)
    after = holder(following, devices)
    before = holder(preceding, devices)
    core = lax.rem(me, 2)
    pair = me // 2
    partner = pair * 2 + (1 - core)
    pairs = segments // 2
    mine = me * BPS

    own_up = pltpu.make_async_copy(up, ups.at[pl.ds(mine, BPS)], loc_sem.at[0])
    own_up.start()
    own_down = pltpu.make_async_copy(down, downs.at[pl.ds(mine, BPS)], loc_sem.at[1])
    own_down.start()
    loads = [
        pltpu.make_async_copy(src, dst, in_sem.at[n])
        for n, (src, dst) in enumerate(
            (
                (neighbours, v_neighbours),
                (rotations, v_rotations),
                (taps, v_taps),
                (bias, v_bias),
                (gain, v_gain),
                (up_bias, v_up_bias),
                (scale, v_scale),
            )
        )
    ]
    for load in loads:
        load.start()
    order = [count - 1, *range(count - 1)]
    half = 2 + (count - 2) // 2
    hid = up_bias.shape[1]
    chans = up.shape[1]
    barrier = pltpu.get_barrier_semaphore()
    new_home = holder(space, devices)

    def greet(where, segment):
        other = jnp.logical_or(where != space, segment != me)

        @pl.when(other)
        def _():
            pl.semaphore_signal(
                barrier, inc=1, device_id=(where, segment), device_id_type=MESH
            )

        return jnp.where(other, 1, 0)

    greetings = 0
    for where in (before, after, preceding, place, following):
        greetings += greet(where, me)
    for step in range(1, segments):
        greetings += greet(space, lax.rem(me + step, segments))
    for segment in range(segments):
        greetings += greet(new_home, segment)

    for load in loads:
        load.wait()
    meta[...] = jnp.full(meta.shape, live_count[0], jnp.int32)
    meta[0:count, 0:8] = bases(v_neighbours[...], v_rotations[...], space, devices, tiles)
    for k in range(BPS):
        small[mine + k, 0 : KS * KS, :] = v_taps[:, k, :].astype(jnp.float32)
        small[mine + k, BIAS : BIAS + 1, :] = v_bias[k : k + 1, :].astype(jnp.float32)
        small[mine + k, GAIN : GAIN + 1, :] = v_gain[k : k + 1, :].astype(jnp.float32)
        small[mine + k, SCALE : SCALE + 1, :] = 0.5 * jnp.exp2(
            v_scale[k : k + 1, :].astype(jnp.float32) * 0.5
        )
        for q in range(hid // chans):
            small[mine + k, UP_BIAS + q : UP_BIAS + q + 1, :] = v_up_bias[
                k : k + 1, q * chans : (q + 1) * chans
            ].astype(jnp.float32)
    def flat(ref):
        return ref.reshape(ref.shape[0] * PS, chans)

    empty = jnp.zeros((CELLS, chans), jnp.float32)
    for turn in range(TURNS):
        at = (turn * tiles + count + 2) * CELLS
        flat(tiles_a)[at : at + CELLS, :] = empty
        flat(tiles_b)[at : at + CELLS, :] = empty
    pl.semaphore_wait(barrier, greetings)

    def send(src, dst, where, segment, send_sem, recv_sem):
        same = jnp.logical_and(where == space, segment == me)

        @pl.when(same)
        def _():
            pltpu.make_async_copy(src, dst, recv_sem).start()

        @pl.when(jnp.logical_not(same))
        def _():
            pltpu.make_async_remote_copy(
                src_ref=src,
                dst_ref=dst,
                send_sem=send_sem,
                recv_sem=recv_sem,
                device_id=(where, segment),
                device_id_type=MESH,
            ).start()

    def sent(src, dst, where, segment, send_sem, recv_sem):
        @pl.when(jnp.logical_not(jnp.logical_and(where == space, segment == me)))
        def _():
            pltpu.make_async_remote_copy(
                src_ref=src,
                dst_ref=dst,
                send_sem=send_sem,
                recv_sem=recv_sem,
                device_id=(where, segment),
                device_id_type=MESH,
            ).wait_send()

    def received(ref, recv_sem):
        pltpu.make_async_copy(ref, ref, recv_sem).wait()

    first = pl.ds(0, CELLS)
    last = pl.ds(rows - CELLS, CELLS)

    def lower(b):
        return edges.at[b, pl.ds(0, CELLS)]

    def upper(b):
        return edges.at[b, pl.ds(CELLS, CELLS)]

    ahead = holder(lax.rem(space + 1, devices), devices)
    behind = holder(lax.rem(space + devices - 1, devices), devices)
    moves = (
        (meta, here, new_home, me, f_send.at[0], f_recv.at[0]),
        (field.at[me, last], lower(0), ahead, me, f_send.at[1], h_recv.at[0, 0]),
        (field.at[me, first], upper(0), behind, me, f_send.at[2], h_recv.at[0, 1]),
        (field.at[me], win.at[0], new_home, me, f_send.at[3], f_recv.at[1]),
    )

    def halo(b, side):
        if side == 0:
            src, dst, to = win.at[b, last], lower(b), after
        else:
            src, dst, to = win.at[b, first], upper(b), before
        return pltpu.make_async_remote_copy(
            src_ref=src,
            dst_ref=dst,
            send_sem=h_send.at[b, side],
            recv_sem=h_recv.at[b, side],
            device_id=(to, me),
            device_id_type=MESH,
        )

    def piece(kind, b, to, send_sem):
        ref = (small, ups, downs)[kind].at[b]
        return pltpu.make_async_remote_copy(
            src_ref=ref,
            dst_ref=ref,
            send_sem=send_sem,
            recv_sem=w_recv.at[kind, b],
            device_id=(space, to),
            device_id_type=MESH,
        )

    def to_partner():
        return [
            piece(kind, mine + k, partner, own_sem.at[k, kind])
            for k in range(BPS)
            for kind in range(3)
        ]

    def to_pairs(k):
        copies = []
        for step in range(1, pairs):
            other = lax.rem(pair + step, pairs) * 2
            at = 3 + (step - 1) * 4
            copies.append(piece(0, mine + k, other, own_sem.at[k, at]))
            copies.append(piece(0, mine + k, other + 1, own_sem.at[k, at + 1]))
            copies.append(piece(1, mine + k, other, own_sem.at[k, at + 2]))
            copies.append(piece(2, mine + k, other + 1, own_sem.at[k, at + 3]))
        return copies

    def forwarded(b, act):
        foreign = b // (2 * BPS) != pair

        @pl.when(jnp.logical_and(foreign, core == 0))
        def _():
            act(piece(1, b, partner, fwd_sem.at[b]))

        @pl.when(jnp.logical_and(foreign, core == 1))
        def _():
            act(piece(2, b, partner, fwd_sem.at[b]))

    def forward(b):
        def act(copy):
            copy.wait_recv()
            copy.start()

        forwarded(b, act)

    def arrive(b):
        owner = b // BPS
        foreign = b // (2 * BPS) != pair

        @pl.when(owner != me)
        def _():
            piece(0, b, partner, fwd_sem.at[b]).wait_recv()

        @pl.when(owner == partner)
        def _():
            piece(1, b, partner, fwd_sem.at[b]).wait_recv()
            piece(2, b, partner, fwd_sem.at[b]).wait_recv()

        @pl.when(jnp.logical_and(foreign, core == 0))
        def _():
            piece(2, b, partner, fwd_sem.at[b]).wait_recv()

        @pl.when(jnp.logical_and(foreign, core == 1))
        def _():
            piece(1, b, partner, fwd_sem.at[b]).wait_recv()

    def outcome(s):
        return (
            win.at[BPS * (s + 1)],
            out.at[me],
            place,
            s,
            o_send.at[s],
            o_recv.at[me],
        )

    def spread(dst, slot, cells):
        dst = flat(dst)
        at = [(turn * tiles + slot) * CELLS for turn in range(TURNS)]
        for i in range(PS):
            row = cells[i * PS : (i + 1) * PS]
            dst[at[0] + i * PS : at[0] + (i + 1) * PS, :] = row
            dst[pl.ds(at[3] + PS - 1 - i, PS, stride=PS), :] = row
        for old, new in ((0, 1), (1, 2)):
            for j in range(PS):
                to = at[new] + (PS - 1 - j) * PS
                dst[to : to + PS, :] = dst[pl.ds(at[old] + j, PS, stride=PS), :]

    def centre(g, i):
        at = g * ROWS + (i + MARGIN) * WIDE + PS
        return slice(at, at + PS)

    def enter(dst, g, cells):
        spread(dst, g, cells)
        for i in range(PS):
            ext[centre(g, i), :] = cells[i * PS : (i + 1) * PS]

    def margins(src, g):
        for d in range(8):
            band_i, band_j = ((0, 0), (0, 1), (0, 2), (1, 0), (1, 2), (2, 0), (2, 1), (2, 2))[d]
            base = links[g, d]
            if band_i == 0:
                lines = [(PS - MARGIN + i, i) for i in range(MARGIN)]
            elif band_i == 1:
                lines = [(i, MARGIN + i) for i in range(PS)]
            else:
                lines = [(i, MARGIN + PS + i) for i in range(MARGIN)]
            for i, to in lines:
                at = g * ROWS + to * WIDE + band_j * PS
                ext[at : at + PS, :] = src[base + i]

    def convolve(b, g):
        total = jnp.broadcast_to(small[b, BIAS : BIAS + 1, :][None], (PS, PS, chans))
        for e in range(KS):
            base = g * ROWS + PS - MARGIN + e
            column = jnp.concatenate(
                [ext[base + i * WIDE : base + i * WIDE + PS, :][None] for i in range(EXT)], axis=0
            )
            for a in range(KS):
                tap = small[b, a * KS + e : a * KS + e + 1, :][None]
                total = total + column[a : a + PS] * tap
        total = total.reshape(CELLS, chans)
        centred = total - jnp.mean(total, axis=-1, keepdims=True)
        variance = jnp.mean(centred * centred, axis=-1, keepdims=True)
        scaled = centred * lax.rsqrt(variance + 1e-06) * small[b, GAIN : GAIN + 1, :]
        return scaled.astype(jnp.bfloat16)

    def group(b, begin, end, dst):
        normed = jnp.concatenate([convolve(b, order[n]) for n in range(begin, end)], axis=0)
        wide = jnp.concatenate(
            [small[b, UP_BIAS + q : UP_BIAS + q + 1, :] for q in range(hid // chans)], axis=1
        )
        hidden = jnp.dot(normed, ups[b], preferred_element_type=jnp.float32) + wide
        hidden = gelu2(hidden).astype(jnp.bfloat16)
        branch = jnp.dot(hidden, downs[b], preferred_element_type=jnp.float32)
        branch = branch * small[b, SCALE : SCALE + 1, :]
        for n in range(begin, end):
            g = order[n]
            alive = jnp.logical_or(g < links[count, 0] - EDGE, g >= count - EDGE)
            alive = jnp.where(alive, 1.0, 0.0)
            old = jnp.concatenate([ext[centre(g, i), :] for i in range(PS)], axis=0)
            state = old + branch[(n - begin) * CELLS : (n - begin + 1) * CELLS]
            state = (state * alive).astype(jnp.bfloat16)
            win[b + 1, g * CELLS : (g + 1) * CELLS, :] = state
            enter(dst, g, state.astype(jnp.float32))

    for move in moves:
        send(*move)
    own_up.wait()
    own_down.wait()

    @pl.when(core == 0)
    def _():
        for copy in to_pairs(0):
            copy.start()

    for copy in to_partner():
        copy.start()
    forward(0)
    received(here, f_recv.at[0])
    table = pltpu.make_async_copy(here, links, loc_sem.at[2])
    table.start()
    received(win.at[0], f_recv.at[1])
    for g in range(count):
        enter(tiles_a, g, win[0, g * CELLS : (g + 1) * CELLS, :].astype(jnp.float32))
    table.wait()

    def layer(s, part):
        b = s * BPS + part
        src, dst = (tiles_a, tiles_b) if part % 2 == 0 else (tiles_b, tiles_a)
        arrive(b)
        for k in range(BPS):
            for c in range(2):
                if k + c and (k + 2 * c - 1) % BPS == part:

                    @pl.when(jnp.logical_and(b == k + 2 * c - 1, core == c))
                    def _():
                        for copy in to_pairs(k):
                            copy.start()

        received(lower(b), h_recv.at[b, 0])
        received(upper(b), h_recv.at[b, 1])
        for side in range(2):
            tile = edges[b, side * CELLS : (side + 1) * CELLS, :].astype(jnp.float32)
            spread(src, count + side, tile)
        for n in range(2):
            margins(src, order[n])
        group(b, 0, 2, dst)

        @pl.when(b < blocks - 1)
        def _():
            halo(b + 1, 0).start()
            halo(b + 1, 1).start()

        for n in range(2, count):
            margins(src, order[n])
        group(b, 2, half, dst)
        group(b, half, count, dst)

        @pl.when(b < blocks - 1)
        def _():
            forward(b + 1)

    def section(s, carry):
        for part in range(BPS):
            layer(s, part)
        send(*outcome(s))
        return carry

    lax.fori_loop(0, segments, section, 0)

    for copy in to_partner() + [copy for k in range(BPS) for copy in to_pairs(k)]:
        copy.wait_send()
    for move in moves:
        sent(*move)

    def drain(b, carry):
        @pl.when(b > 0)
        def _():
            halo(b, 0).wait_send()
            halo(b, 1).wait_send()

        forwarded(b, lambda copy: copy.wait_send())
        return carry

    lax.fori_loop(0, blocks, drain, 0)
    for s in range(segments):
        sent(*outcome(s))
    for member in range(segments):
        received(out.at[member], o_recv.at[member])


def body(
    field,
    depth_kernel,
    depth_bias,
    norm_gain,
    up_weight,
    up_bias,
    down_weight,
    scale_exponent,
    live_count,
    neighbours,
    rotations,
):
    members, count = field.shape[:2]
    chans = field.shape[-1]
    hid = up_weight.shape[-1]
    segments = lax.axis_size("segment")
    devices = lax.axis_size("space")
    blocks = segments * BPS
    assert members == segments and segments % 2 == 0 and count % 2 == 0
    assert BPS % 2 == 0 and devices % 2 == 0
    pairs = segments // 2
    metas = count + 8
    smalls = -(-(UP_BIAS + hid // chans) // 8) * 8
    smem = pl.BlockSpec(memory_space=pltpu.SMEM)
    hbm = pl.BlockSpec(memory_space=pl.ANY)
    dma = pltpu.SemaphoreType.DMA
    out = pl.pallas_call(
        functools.partial(kernel, segments, devices, blocks),
        out_shape=jax.ShapeDtypeStruct((members, count * CELLS, chans), jnp.bfloat16),
        in_specs=[hbm] * 8 + [smem] + [hbm] * 2,
        out_specs=pl.BlockSpec(memory_space=pl.ANY),
        scratch_shapes=[
            pltpu.VMEM((KS * KS, BPS, chans), jnp.bfloat16),
            pltpu.VMEM((BPS, chans), jnp.bfloat16),
            pltpu.VMEM((BPS, chans), jnp.bfloat16),
            pltpu.VMEM((BPS, hid), jnp.bfloat16),
            pltpu.VMEM((BPS, chans), jnp.int32),
            pltpu.VMEM(neighbours.shape, jnp.int32),
            pltpu.VMEM(rotations.shape, jnp.int32),
            pltpu.VMEM((metas, chans), jnp.int32),
            pltpu.VMEM((metas, chans), jnp.int32),
            pltpu.SMEM((metas, chans), jnp.int32),
            pltpu.VMEM((blocks + 1, count * CELLS, chans), jnp.bfloat16),
            pltpu.VMEM((blocks, 2 * CELLS, chans), jnp.bfloat16),
            pltpu.VMEM((blocks, chans, hid), jnp.bfloat16),
            pltpu.VMEM((blocks, hid, chans), jnp.bfloat16),
            pltpu.VMEM((blocks, smalls, chans), jnp.float32),
            pltpu.VMEM((TURNS * (count + 3) * PS, PS, chans), jnp.float32),
            pltpu.VMEM((TURNS * (count + 3) * PS, PS, chans), jnp.float32),
            pltpu.VMEM((count * ROWS, chans), jnp.float32),
            dma((3,)),
            dma((BPS, 3 + 4 * (pairs - 1))),
            dma((3, blocks)),
            dma((blocks,)),
            dma((blocks, 2)),
            dma((blocks, 2)),
            dma((4,)),
            dma((2,)),
            dma((segments,)),
            dma((members,)),
            dma((7,)),
        ],
        compiler_params=pltpu.CompilerParams(
            collective_id=0, has_side_effects=True, vmem_limit_bytes=60 * 2**20
        ),
    )(
        field.reshape(members, count * CELLS, chans),
        jnp.transpose(depth_kernel, (1, 0, 2)),
        depth_bias,
        norm_gain,
        up_weight,
        up_bias,
        down_weight,
        scale_exponent,
        live_count,
        neighbours,
        rotations,
    )
    return out.reshape((1,) + field.shape)


def solution(mesh):
    in_specs = (
        P(None, "space", None, None, None),
        P("segment", None, None),
        P("segment", None),
        P("segment", None),
        P("segment", None, None),
        P("segment", None),
        P("segment", None, None),
        P("segment", None),
        P("space"),
        P("space", None),
        P("space", None),
    )
    out_specs = P("segment", None, "space", None, None, None)
    return jax.shard_map(body, mesh=mesh, in_specs=in_specs, out_specs=out_specs, check_vma=False)
```

time: 55.6 us -> 50.5 us (0.908)
  the two profiles are of different devices: /device:TPU:0 before, /device:TPU:31 now
where the time goes in v1:
time: 50.5 us; the launch traced here: 50.3 us
  Pallas kernels  47.7 us (94%)
  local copies, waits for them, and re-layouts  1.87 us (4%)
  between operations  0.66 us (1%)
    pallas_call x1, Pallas kernels, body(): pl.pallas_call(functools.partial(kernel, segments, devices, blocks), out_...  47.7 us
    unnamed x1, local copies, waits for them, and re-layouts  1.87 us

profile of v1, /device:TPU:31, one launch (start us, length us, event | category | flops | bytes accessed | tf_op | source)
XLA Modules:
  0.0 50.3 jit_solution(3026917775010175786)
XLA Ops:
  0.7 47.7 %shard_map.109 = bf16[4,512,128]{2,1,0:T(8,128)(2,1)} custom-call(bf16[4,512,128]{2,1,0:T(8,128)(2,1)} %bitcast.4, bf16[49,2,128]{2,1,0:T(2,128)(2,1)} %bitcast.5, bf16[2,128]{1,0:T(2,128)(2,1)} %bias.1, bf16[2,128]{1,0:T(2,128)(2,1)} %gain.1, bf16[2,128,512]{2,1,0:T(8,128)(2,1)} %up.1, bf16[2,512]{1,0:T(2,128)(2,1)} %up_bias.1, bf16[2,512,128]{2,1,0:T(8,128)(2,1)} %down.1, ...), custom_call_target="tpu_custom_call" | custom-call | tf_op jit(solution)/shard_map/pallas_call | solution.py:519
  48.4 1.9 %copy.14 = bf16[1,4,8,8,8,128]{5,4,3,2,1,0:T(8,128)(2,1)} copy(bf16[1,4,8,8,8,128]{5,4,3,2,1,0:T(8,128)(2,1)} %bitcast.3) | data formatting | bytes 1048576

commit v2 on v1

--- a/solution.py
+++ b/solution.py
@@ -16,15 +16,14 @@
 CELLS = PS * PS
 EXT = PS + 2 * MARGIN
 WIDE = 3 * PS
-ROWS = EXT * WIDE
 TURNS = 4
 MESH = pl.DeviceIdType.MESH
 HOLDERS = {8: (0, 1, 2, 3, 5, 7, 6, 4)}
 
-BIAS = KS * KS
-GAIN = BIAS + 1
-SCALE = GAIN + 1
-UP_BIAS = SCALE + 1
+BIAS = 0
+GAIN = 1
+SCALE = 2
+UP_BIAS = 3
 
 
 def bases(neighbours, rotations, place, devices, tiles):
@@ -119,6 +118,28 @@
     pairs = segments // 2
     mine = me * BPS
 
+    barrier = pltpu.get_barrier_semaphore()
+    new_home = holder(space, devices)
+
+    def greet(where, segment):
+        other = jnp.logical_or(where != space, segment != me)
+
+        @pl.when(other)
+        def _():
+            pl.semaphore_signal(
+                barrier, inc=1, device_id=(where, segment), device_id_type=MESH
+            )
+
+        return jnp.where(other, 1, 0)
+
+    greetings = 0
+    for where in (before, after, preceding, place, following):
+        greetings += greet(where, me)
+    for step in range(1, segments):
+        greetings += greet(space, lax.rem(me + step, segments))
+    for segment in range(segments):
+        greetings += greet(new_home, segment)
+
     own_up = pltpu.make_async_copy(up, ups.at[pl.ds(mine, BPS)], loc_sem.at[0])
     own_up.start()
     own_down = pltpu.make_async_copy(down, downs.at[pl.ds(mine, BPS)], loc_sem.at[1])
@@ -143,43 +164,25 @@
     half = 2 + (count - 2) // 2
     hid = up_bias.shape[1]
     chans = up.shape[1]
-    barrier = pltpu.get_barrier_semaphore()
-    new_home = holder(space, devices)
-
-    def greet(where, segment):
-        other = jnp.logical_or(where != space, segment != me)
-
-        @pl.when(other)
-        def _():
-            pl.semaphore_signal(
-                barrier, inc=1, device_id=(where, segment), device_id_type=MESH
-            )
-
-        return jnp.where(other, 1, 0)
-
-    greetings = 0
-    for where in (before, after, preceding, place, following):
-        greetings += greet(where, me)
-    for step in range(1, segments):
-        greetings += greet(space, lax.rem(me + step, segments))
-    for segment in range(segments):
-        greetings += greet(new_home, segment)
-
     for load in loads:
         load.wait()
     meta[...] = jnp.full(meta.shape, live_count[0], jnp.int32)
     meta[0:count, 0:8] = bases(v_neighbours[...], v_rotations[...], space, devices, tiles)
     for k in range(BPS):
-        small[mine + k, 0 : KS * KS, :] = v_taps[:, k, :].astype(jnp.float32)
-        small[mine + k, BIAS : BIAS + 1, :] = v_bias[k : k + 1, :].astype(jnp.float32)
-        small[mine + k, GAIN : GAIN + 1, :] = v_gain[k : k + 1, :].astype(jnp.float32)
-        small[mine + k, SCALE : SCALE + 1, :] = 0.5 * jnp.exp2(
+        for row in range(KS):
+            small[mine + k, row, 0:KS, :] = v_taps[
+                row * KS : (row + 1) * KS, k, :
+            ].astype(jnp.float32)
+        small[mine + k, KS, BIAS : BIAS + 1, :] = v_bias[k : k + 1, :].astype(jnp.float32)
+        small[mine + k, KS, GAIN : GAIN + 1, :] = v_gain[k : k + 1, :].astype(jnp.float32)
+        small[mine + k, KS, SCALE : SCALE + 1, :] = 0.5 * jnp.exp2(
             v_scale[k : k + 1, :].astype(jnp.float32) * 0.5
         )
         for q in range(hid // chans):
-            small[mine + k, UP_BIAS + q : UP_BIAS + q + 1, :] = v_up_bias[
+            small[mine + k, KS, UP_BIAS + q : UP_BIAS + q + 1, :] = v_up_bias[
                 k : k + 1, q * chans : (q + 1) * chans
             ].astype(jnp.float32)
+
     def flat(ref):
         return ref.reshape(ref.shape[0] * PS, chans)
 
@@ -323,14 +326,17 @@
         def _():
             piece(1, b, partner, fwd_sem.at[b]).wait_recv()
 
-    def outcome(s):
+    chunks = ((count - 1, 1), (0, 1), (1, half - 2), (half - 1, count - half))
+
+    def outcome(s, n):
+        at = pl.ds(chunks[n][0] * CELLS, chunks[n][1] * CELLS)
         return (
-            win.at[BPS * (s + 1)],
-            out.at[me],
+            win.at[BPS * (s + 1), at],
+            out.at[me, at],
             place,
             s,
-            o_send.at[s],
-            o_recv.at[me],
+            o_send.at[s, n],
+            o_recv.at[me, n],
         )
 
     def spread(dst, slot, cells):
@@ -345,14 +351,12 @@
                 to = at[new] + (PS - 1 - j) * PS
                 dst[to : to + PS, :] = dst[pl.ds(at[old] + j, PS, stride=PS), :]
 
-    def centre(g, i):
-        at = g * ROWS + (i + MARGIN) * WIDE + PS
-        return slice(at, at + PS)
+    def middle(g):
+        return (slice(g * EXT + MARGIN, g * EXT + MARGIN + PS), slice(PS, 2 * PS))
 
     def enter(dst, g, cells):
         spread(dst, g, cells)
-        for i in range(PS):
-            ext[centre(g, i), :] = cells[i * PS : (i + 1) * PS]
+        ext[middle(g)] = cells.reshape(PS, PS, chans)
 
     def margins(src, g):
         for d in range(8):
@@ -365,43 +369,51 @@
             else:
                 lines = [(i, MARGIN + PS + i) for i in range(MARGIN)]
             for i, to in lines:
-                at = g * ROWS + to * WIDE + band_j * PS
-                ext[at : at + PS, :] = src[base + i]
-
-    def convolve(b, g):
-        total = jnp.broadcast_to(small[b, BIAS : BIAS + 1, :][None], (PS, PS, chans))
-        for e in range(KS):
-            base = g * ROWS + PS - MARGIN + e
-            column = jnp.concatenate(
-                [ext[base + i * WIDE : base + i * WIDE + PS, :][None] for i in range(EXT)], axis=0
-            )
-            for a in range(KS):
-                tap = small[b, a * KS + e : a * KS + e + 1, :][None]
-                total = total + column[a : a + PS] * tap
-        total = total.reshape(CELLS, chans)
+                ext[g * EXT + to, band_j * PS : (band_j + 1) * PS, :] = src[base + i]
+
+    def convolve(b, places):
+        def line(a, total):
+            for e in range(KS):
+                window = jnp.concatenate(
+                    [
+                        ext[pl.ds(g * EXT + a, PS), PS - MARGIN + e : 2 * PS - MARGIN + e, :]
+                        for g in places
+                    ],
+                    axis=0,
+                )
+                total = total + window * small[b, a, e : e + 1, :][None]
+            return total
+
+        start = small[b, KS, BIAS : BIAS + 1, :][None]
+        start = jnp.broadcast_to(start, (len(places) * PS, PS, chans))
+        total = lax.fori_loop(0, KS, line, start).reshape(-1, chans)
         centred = total - jnp.mean(total, axis=-1, keepdims=True)
         variance = jnp.mean(centred * centred, axis=-1, keepdims=True)
-        scaled = centred * lax.rsqrt(variance + 1e-06) * small[b, GAIN : GAIN + 1, :]
+        scaled = centred * lax.rsqrt(variance + 1e-06) * small[b, KS, GAIN : GAIN + 1, :]
         return scaled.astype(jnp.bfloat16)
 
-    def group(b, begin, end, dst):
-        normed = jnp.concatenate([convolve(b, order[n]) for n in range(begin, end)], axis=0)
+    def group(b, begin, end):
+        normed = convolve(b, order[begin:end])
         wide = jnp.concatenate(
-            [small[b, UP_BIAS + q : UP_BIAS + q + 1, :] for q in range(hid // chans)], axis=1
+            [small[b, KS, UP_BIAS + q : UP_BIAS + q + 1, :] for q in range(hid // chans)], axis=1
         )
         hidden = jnp.dot(normed, ups[b], preferred_element_type=jnp.float32) + wide
         hidden = gelu2(hidden).astype(jnp.bfloat16)
         branch = jnp.dot(hidden, downs[b], preferred_element_type=jnp.float32)
-        branch = branch * small[b, SCALE : SCALE + 1, :]
+        branch = branch * small[b, KS, SCALE : SCALE + 1, :]
         for n in range(begin, end):
             g = order[n]
             alive = jnp.logical_or(g < links[count, 0] - EDGE, g >= count - EDGE)
             alive = jnp.where(alive, 1.0, 0.0)
-            old = jnp.concatenate([ext[centre(g, i), :] for i in range(PS)], axis=0)
+            old = ext[middle(g)].reshape(CELLS, chans)
             state = old + branch[(n - begin) * CELLS : (n - begin + 1) * CELLS]
             state = (state * alive).astype(jnp.bfloat16)
             win[b + 1, g * CELLS : (g + 1) * CELLS, :] = state
-            enter(dst, g, state.astype(jnp.float32))
+
+    def settle(b, begin, end, dst):
+        for n in range(begin, end):
+            g = order[n]
+            enter(dst, g, win[b + 1, g * CELLS : (g + 1) * CELLS, :].astype(jnp.float32))
 
     for move in moves:
         send(*move)
@@ -444,17 +456,27 @@
             spread(src, count + side, tile)
         for n in range(2):
             margins(src, order[n])
-        group(b, 0, 2, dst)
+        group(b, 0, 2)
 
         @pl.when(b < blocks - 1)
         def _():
             halo(b + 1, 0).start()
             halo(b + 1, 1).start()
 
+        ends = part == BPS - 1
+        if ends:
+            send(*outcome(s, 0))
+            send(*outcome(s, 1))
+        settle(b, 0, 2, dst)
         for n in range(2, count):
             margins(src, order[n])
-        group(b, 2, half, dst)
-        group(b, half, count, dst)
+        group(b, 2, half)
+        if ends:
+            send(*outcome(s, 2))
+        group(b, half, count)
+        if ends:
+            send(*outcome(s, 3))
+        settle(b, 2, count, dst)
 
         @pl.when(b < blocks - 1)
         def _():
@@ -463,7 +485,6 @@
     def section(s, carry):
         for part in range(BPS):
             layer(s, part)
-        send(*outcome(s))
         return carry
 
     lax.fori_loop(0, segments, section, 0)
@@ -484,9 +505,11 @@
 
     lax.fori_loop(0, blocks, drain, 0)
     for s in range(segments):
-        sent(*outcome(s))
+        for n in range(len(chunks)):
+            sent(*outcome(s, n))
     for member in range(segments):
-        received(out.at[member], o_recv.at[member])
+        for n, (start, size) in enumerate(chunks):
+            received(out.at[member, pl.ds(start * CELLS, size * CELLS)], o_recv.at[member, n])
 
 
 def body(
@@ -512,7 +535,7 @@
     assert BPS % 2 == 0 and devices % 2 == 0
     pairs = segments // 2
     metas = count + 8
-    smalls = -(-(UP_BIAS + hid // chans) // 8) * 8
+    assert UP_BIAS + hid // chans <= PS
     smem = pl.BlockSpec(memory_space=pltpu.SMEM)
     hbm = pl.BlockSpec(memory_space=pl.ANY)
     dma = pltpu.SemaphoreType.DMA
@@ -536,10 +559,10 @@
             pltpu.VMEM((blocks, 2 * CELLS, chans), jnp.bfloat16),
             pltpu.VMEM((blocks, chans, hid), jnp.bfloat16),
             pltpu.VMEM((blocks, hid, chans), jnp.bfloat16),
-            pltpu.VMEM((blocks, smalls, chans), jnp.float32),
+            pltpu.VMEM((blocks, KS + 1, PS, chans), jnp.float32),
             pltpu.VMEM((TURNS * (count + 3) * PS, PS, chans), jnp.float32),
             pltpu.VMEM((TURNS * (count + 3) * PS, PS, chans), jnp.float32),
-            pltpu.VMEM((count * ROWS, chans), jnp.float32),
+            pltpu.VMEM((count * EXT, WIDE, chans), jnp.float32),
             dma((3,)),
             dma((BPS, 3 + 4 * (pairs - 1))),
             dma((3, blocks)),
@@ -548,8 +571,8 @@
             dma((blocks, 2)),
             dma((4,)),
             dma((2,)),
-            dma((segments,)),
-            dma((members,)),
+            dma((segments, 4)),
+            dma((members, 4)),
             dma((7,)),
         ],
         compiler_params=pltpu.CompilerParams(

time: 50.5 us -> 50 us (0.990)
  no operation moved by 1% of the time
where the time goes in v2:
time: 50 us; the launch traced here: 49.8 us
  Pallas kernels  47.2 us (94%)
  local copies, waits for them, and re-layouts  1.87 us (4%)
  between operations  0.66 us (1%)
    pallas_call x1, Pallas kernels, body(): pl.pallas_call(functools.partial(kernel, segments, devices, blocks), out_...  47.2 us
    unnamed x1, local copies, waits for them, and re-layouts  1.87 us

profile of v2, /device:TPU:31, one launch (start us, length us, event | category | flops | bytes accessed | tf_op | source)
XLA Modules:
  0.0 49.8 jit_solution(9081428946529579389)
XLA Ops:
  0.7 47.2 %shard_map.109 = bf16[4,512,128]{2,1,0:T(8,128)(2,1)} custom-call(bf16[4,512,128]{2,1,0:T(8,128)(2,1)} %bitcast.4, bf16[49,2,128]{2,1,0:T(2,128)(2,1)} %bitcast.5, bf16[2,128]{1,0:T(2,128)(2,1)} %bias.1, bf16[2,128]{1,0:T(2,128)(2,1)} %gain.1, bf16[2,128,512]{2,1,0:T(8,128)(2,1)} %up.1, bf16[2,512]{1,0:T(2,128)(2,1)} %up_bias.1, bf16[2,512,128]{2,1,0:T(8,128)(2,1)} %down.1, ...), custom_call_target="tpu_custom_call" | custom-call | tf_op jit(solution)/shard_map/pallas_call | solution.py:542
  47.9 1.9 %copy.14 = bf16[1,4,8,8,8,128]{5,4,3,2,1,0:T(8,128)(2,1)} copy(bf16[1,4,8,8,8,128]{5,4,3,2,1,0:T(8,128)(2,1)} %bitcast.3) | data formatting | bytes 1048576

commit v3 on v2

--- a/solution.py
+++ b/solution.py
@@ -541,9 +541,9 @@
     dma = pltpu.SemaphoreType.DMA
     out = pl.pallas_call(
         functools.partial(kernel, segments, devices, blocks),
-        out_shape=jax.ShapeDtypeStruct((members, count * CELLS, chans), jnp.bfloat16),
+        out_shape=pltpu.VMEM((members, count * CELLS, chans), jnp.bfloat16),
         in_specs=[hbm] * 8 + [smem] + [hbm] * 2,
-        out_specs=pl.BlockSpec(memory_space=pl.ANY),
+        out_specs=pl.BlockSpec(memory_space=pltpu.VMEM),
         scratch_shapes=[
             pltpu.VMEM((KS * KS, BPS, chans), jnp.bfloat16),
             pltpu.VMEM((BPS, chans), jnp.bfloat16),

time: 50 us -> 48.8 us (0.976)
  local copies, waits for them, and re-layouts: 1.87 us -> 0.8 us
    unnamed x1, local copies, waits for them, and re-layouts: 1.87 us -> 0.8 us
where the time goes in v3:
time: 48.8 us; the launch traced here: 48.6 us
  Pallas kernels  47.1 us (97%)
  local copies, waits for them, and re-layouts  0.8 us (2%)
  between operations  0.66 us (1%)
    pallas_call x1, Pallas kernels, body(): pl.pallas_call(functools.partial(kernel, segments, devices, blocks), out_...  47.1 us

profile of v3, /device:TPU:31, one launch (start us, length us, event | category | flops | bytes accessed | tf_op | source)
XLA Modules:
  0.0 48.6 jit_solution(13574828270813671431)
XLA Ops:
  0.7 47.1 %shard_map.109 = bf16[4,512,128]{2,1,0:T(8,128)(2,1)S(1)} custom-call(bf16[4,512,128]{2,1,0:T(8,128)(2,1)} %bitcast.4, bf16[49,2,128]{2,1,0:T(2,128)(2,1)} %bitcast.5, bf16[2,128]{1,0:T(2,128)(2,1)} %bias.1, bf16[2,128]{1,0:T(2,128)(2,1)} %gain.1, bf16[2,128,512]{2,1,0:T(8,128)(2,1)} %up.1, bf16[2,512]{1,0:T(2,128)(2,1)} %up_bias.1, ...), custom_call_target="tpu_custom_call" | custom-call | tf_op jit(solution)/shard_map/pallas_call | solution.py:542
  47.8 0.8 %copy.13 = bf16[1,4,8,8,8,128]{5,4,3,2,1,0:T(8,128)(2,1)} copy(bf16[1,4,8,8,8,128]{5,4,3,2,1,0:T(8,128)(2,1)S(1)} %bitcast.3) | data formatting | bytes 1048576

commit v4 on v3

--- a/solution.py
+++ b/solution.py
@@ -18,7 +18,7 @@
 WIDE = 3 * PS
 TURNS = 4
 MESH = pl.DeviceIdType.MESH
-HOLDERS = {8: (0, 1, 2, 3, 5, 7, 6, 4)}
+HOLDERS = {8: (2, 0, 1, 3, 5, 7, 6, 4)}
 
 BIAS = 0
 GAIN = 1
@@ -282,21 +282,28 @@
             other = lax.rem(pair + step, pairs) * 2
             at = 3 + (step - 1) * 4
             copies.append(piece(0, mine + k, other, own_sem.at[k, at]))
-            copies.append(piece(0, mine + k, other + 1, own_sem.at[k, at + 1]))
             copies.append(piece(1, mine + k, other, own_sem.at[k, at + 2]))
             copies.append(piece(2, mine + k, other + 1, own_sem.at[k, at + 3]))
         return copies
 
+    def turn_of(k):
+        if k == 0:
+            late = jnp.where(core == 0, 1, 4)
+        else:
+            late = jnp.where(core == 0, 2, 5)
+        return jnp.where(pair == 0, jnp.where(core == 0, -1, k + 1), 2 * BPS * (pair - 1) + late)
+
     def forwarded(b, act):
         foreign = b // (2 * BPS) != pair
 
         @pl.when(jnp.logical_and(foreign, core == 0))
         def _():
-            act(piece(1, b, partner, fwd_sem.at[b]))
+            act(piece(0, b, partner, fwd_sem.at[1, b]))
+            act(piece(1, b, partner, fwd_sem.at[0, b]))
 
         @pl.when(jnp.logical_and(foreign, core == 1))
         def _():
-            act(piece(2, b, partner, fwd_sem.at[b]))
+            act(piece(2, b, partner, fwd_sem.at[0, b]))
 
     def forward(b):
         def act(copy):
@@ -309,22 +316,24 @@
         owner = b // BPS
         foreign = b // (2 * BPS) != pair
 
-        @pl.when(owner != me)
-        def _():
-            piece(0, b, partner, fwd_sem.at[b]).wait_recv()
+        relayed = jnp.logical_and(foreign, core == 0)
+
+        @pl.when(jnp.logical_and(owner != me, jnp.logical_not(relayed)))
+        def _():
+            piece(0, b, partner, fwd_sem.at[0, b]).wait_recv()
 
         @pl.when(owner == partner)
         def _():
-            piece(1, b, partner, fwd_sem.at[b]).wait_recv()
-            piece(2, b, partner, fwd_sem.at[b]).wait_recv()
+            piece(1, b, partner, fwd_sem.at[0, b]).wait_recv()
+            piece(2, b, partner, fwd_sem.at[0, b]).wait_recv()
 
         @pl.when(jnp.logical_and(foreign, core == 0))
         def _():
-            piece(2, b, partner, fwd_sem.at[b]).wait_recv()
+            piece(2, b, partner, fwd_sem.at[0, b]).wait_recv()
 
         @pl.when(jnp.logical_and(foreign, core == 1))
         def _():
-            piece(1, b, partner, fwd_sem.at[b]).wait_recv()
+            piece(1, b, partner, fwd_sem.at[0, b]).wait_recv()
 
     chunks = ((count - 1, 1), (0, 1), (1, half - 2), (half - 1, count - half))
 
@@ -420,14 +429,23 @@
     own_up.wait()
     own_down.wait()
 
-    @pl.when(core == 0)
+    opening = me == 0
+
+    @pl.when(opening)
     def _():
         for copy in to_pairs(0):
             copy.start()
 
     for copy in to_partner():
         copy.start()
+
+    @pl.when(opening)
+    def _():
+        for copy in to_pairs(1):
+            copy.start()
+
     forward(0)
+
     received(here, f_recv.at[0])
     table = pltpu.make_async_copy(here, links, loc_sem.at[2])
     table.start()
@@ -441,13 +459,11 @@
         src, dst = (tiles_a, tiles_b) if part % 2 == 0 else (tiles_b, tiles_a)
         arrive(b)
         for k in range(BPS):
-            for c in range(2):
-                if k + c and (k + 2 * c - 1) % BPS == part:
-
-                    @pl.when(jnp.logical_and(b == k + 2 * c - 1, core == c))
-                    def _():
-                        for copy in to_pairs(k):
-                            copy.start()
+
+            @pl.when(b == turn_of(k))
+            def _():
+                for copy in to_pairs(k):
+                    copy.start()
 
         received(lower(b), h_recv.at[b, 0])
         received(upper(b), h_recv.at[b, 1])
@@ -489,8 +505,9 @@
 
     lax.fori_loop(0, segments, section, 0)
 
-    for copy in to_partner() + [copy for k in range(BPS) for copy in to_pairs(k)]:
+    for copy in to_partner() + to_pairs(0) + to_pairs(1):
         copy.wait_send()
+
     for move in moves:
         sent(*move)
 
@@ -532,7 +549,7 @@
     devices = lax.axis_size("space")
     blocks = segments * BPS
     assert members == segments and segments % 2 == 0 and count % 2 == 0
-    assert BPS % 2 == 0 and devices % 2 == 0
+    assert BPS == 2 and devices % 2 == 0
     pairs = segments // 2
     metas = count + 8
     assert UP_BIAS + hid // chans <= PS
@@ -566,7 +583,7 @@
             dma((3,)),
             dma((BPS, 3 + 4 * (pairs - 1))),
             dma((3, blocks)),
-            dma((blocks,)),
+            dma((2, blocks)),
             dma((blocks, 2)),
             dma((blocks, 2)),
             dma((4,)),

time: 48.8 us -> 46.8 us (0.959)
  the two profiles are of different devices: /device:TPU:31 before, /device:TPU:0 now
where the time goes in v4:
time: 46.8 us; the launch traced here: 46.3 us
  Pallas kernels  44.8 us (96%)
  local copies, waits for them, and re-layouts  0.8 us (2%)
  between operations  0.66 us (1%)
    pallas_call x1, Pallas kernels, body(): pl.pallas_call(functools.partial(kernel, segments, devices, blocks), out_...  44.8 us

profile of v4, /device:TPU:0, one launch (start us, length us, event | category | flops | bytes accessed | tf_op | source)
XLA Modules:
  0.0 46.3 jit_solution(8658141919352131600)
XLA Ops:
  0.7 44.8 %shard_map.109 = bf16[4,512,128]{2,1,0:T(8,128)(2,1)S(1)} custom-call(bf16[4,512,128]{2,1,0:T(8,128)(2,1)} %bitcast.4, bf16[49,2,128]{2,1,0:T(2,128)(2,1)} %bitcast.5, bf16[2,128]{1,0:T(2,128)(2,1)} %bias.1, bf16[2,128]{1,0:T(2,128)(2,1)} %gain.1, bf16[2,128,512]{2,1,0:T(8,128)(2,1)} %up.1, bf16[2,512]{1,0:T(2,128)(2,1)} %up_bias.1, ...), custom_call_target="tpu_custom_call" | custom-call | tf_op jit(solution)/shard_map/pallas_call | solution.py:559
  45.5 0.8 %copy.13 = bf16[1,4,8,8,8,128]{5,4,3,2,1,0:T(8,128)(2,1)} copy(bf16[1,4,8,8,8,128]{5,4,3,2,1,0:T(8,128)(2,1)S(1)} %bitcast.3) | data formatting | bytes 1048576

commit v5 on v4

--- a/solution.py
+++ b/solution.py
@@ -322,6 +322,10 @@
         def _():
             piece(0, b, partner, fwd_sem.at[0, b]).wait_recv()
 
+    def arrive_wide(b):
+        owner = b // BPS
+        foreign = b // (2 * BPS) != pair
+
         @pl.when(owner == partner)
         def _():
             piece(1, b, partner, fwd_sem.at[0, b]).wait_recv()
@@ -403,6 +407,8 @@
 
     def group(b, begin, end):
         normed = convolve(b, order[begin:end])
+        if begin == 0:
+            arrive_wide(b)
         wide = jnp.concatenate(
             [small[b, KS, UP_BIAS + q : UP_BIAS + q + 1, :] for q in range(hid // chans)], axis=1
         )

time: 46.8 us -> 46.2 us (0.987)
  Pallas kernels: 44.8 us -> 44.1 us
    pallas_call x1, Pallas kernels: 44.8 us -> 44.1 us  [body(): pl.pallas_call(functools.partial(kernel, segments, devices, blocks), out_...]
where the time goes in v5:
time: 46.2 us; the launch traced here: 45.5 us
  Pallas kernels  44.1 us (95%)
  local copies, waits for them, and re-layouts  0.8 us (2%)
  between operations  0.66 us (1%)
    pallas_call x1, Pallas kernels, body(): pl.pallas_call(functools.partial(kernel, segments, devices, blocks), out_...  44.1 us

profile of v5, /device:TPU:0, one launch (start us, length us, event | category | flops | bytes accessed | tf_op | source)
XLA Modules:
  0.0 45.5 jit_solution(14848713059337148434)
XLA Ops:
  0.7 44.1 %shard_map.109 = bf16[4,512,128]{2,1,0:T(8,128)(2,1)S(1)} custom-call(bf16[4,512,128]{2,1,0:T(8,128)(2,1)} %bitcast.4, bf16[49,2,128]{2,1,0:T(2,128)(2,1)} %bitcast.5, bf16[2,128]{1,0:T(2,128)(2,1)} %bias.1, bf16[2,128]{1,0:T(2,128)(2,1)} %gain.1, bf16[2,128,512]{2,1,0:T(8,128)(2,1)} %up.1, bf16[2,512]{1,0:T(2,128)(2,1)} %up_bias.1, ...), custom_call_target="tpu_custom_call" | custom-call | tf_op jit(solution)/shard_map/pallas_call | solution.py:565
  44.7 0.8 %copy.13 = bf16[1,4,8,8,8,128]{5,4,3,2,1,0:T(8,128)(2,1)} copy(bf16[1,4,8,8,8,128]{5,4,3,2,1,0:T(8,128)(2,1)S(1)} %bitcast.3) | data formatting | bytes 1048576

commit v6 on v5

--- a/solution.py
+++ b/solution.py
@@ -291,7 +291,7 @@
             late = jnp.where(core == 0, 1, 4)
         else:
             late = jnp.where(core == 0, 2, 5)
-        return jnp.where(pair == 0, jnp.where(core == 0, -1, k + 1), 2 * BPS * (pair - 1) + late)
+        return jnp.where(pair == 0, -1, 2 * BPS * (pair - 1) + late)
 
     def forwarded(b, act):
         foreign = b // (2 * BPS) != pair
@@ -495,14 +495,21 @@
         group(b, 2, half)
         if ends:
             send(*outcome(s, 2))
+        @pl.when(b < blocks - 1)
+        def _():
+            forward(b + 1)
+
         group(b, half, count)
+        for k in range(BPS):
+
+            @pl.when(jnp.logical_and(me == 1, b == k))
+            def _():
+                for copy in to_pairs(k):
+                    copy.start()
+
         if ends:
             send(*outcome(s, 3))
         settle(b, 2, count, dst)
-
-        @pl.when(b < blocks - 1)
-        def _():
-            forward(b + 1)
 
     def section(s, carry):
         for part in range(BPS):

time: 46.2 us -> 44.2 us (0.957); the launches traced: 45.5 us -> 44 us
  Pallas kernels: 44.1 us -> 42.5 us
    pallas_call x1, Pallas kernels: 44.1 us -> 42.5 us  [body(): pl.pallas_call(functools.partial(kernel, segments, devices, blocks), out_...]
where the time goes in v6:
time: 44.2 us; the launch traced here: 44 us
  Pallas kernels  42.5 us (96%)
  local copies, waits for them, and re-layouts  0.8 us (2%)
  between operations  0.66 us (1%)
    pallas_call x1, Pallas kernels, body(): pl.pallas_call(functools.partial(kernel, segments, devices, blocks), out_...  42.5 us

profile of v6, /device:TPU:0, one launch (start us, length us, event | category | flops | bytes accessed | tf_op | source)
XLA Modules:
  0.0 44.0 jit_solution(14220051985178376024)
XLA Ops:
  0.7 42.5 %shard_map.109 = bf16[4,512,128]{2,1,0:T(8,128)(2,1)S(1)} custom-call(bf16[4,512,128]{2,1,0:T(8,128)(2,1)} %bitcast.4, bf16[49,2,128]{2,1,0:T(2,128)(2,1)} %bitcast.5, bf16[2,128]{1,0:T(2,128)(2,1)} %bias.1, bf16[2,128]{1,0:T(2,128)(2,1)} %gain.1, bf16[2,128,512]{2,1,0:T(8,128)(2,1)} %up.1, bf16[2,512]{1,0:T(2,128)(2,1)} %up_bias.1, ...), custom_call_target="tpu_custom_call" | custom-call | tf_op jit(solution)/shard_map/pallas_call | solution.py:572
  43.2 0.8 %copy.13 = bf16[1,4,8,8,8,128]{5,4,3,2,1,0:T(8,128)(2,1)} copy(bf16[1,4,8,8,8,128]{5,4,3,2,1,0:T(8,128)(2,1)S(1)} %bitcast.3) | data formatting | bytes 1048576

commit v7 on v6

--- a/solution.py
+++ b/solution.py
@@ -430,7 +430,7 @@
             g = order[n]
             enter(dst, g, win[b + 1, g * CELLS : (g + 1) * CELLS, :].astype(jnp.float32))
 
-    for move in moves:
+    for move in moves[:3]:
         send(*move)
     own_up.wait()
     own_down.wait()
@@ -442,6 +442,7 @@
         for copy in to_pairs(0):
             copy.start()
 
+    send(*moves[3])
     for copy in to_partner():
         copy.start()
 

time: 44.2 us -> 44.2 us (level)
  no operation moved by 1% of the time
where the time goes in v7:
time: 44.2 us; the launch traced here: 44 us
  Pallas kernels  42.5 us (96%)
  local copies, waits for them, and re-layouts  0.8 us (2%)
  between operations  0.66 us (1%)
    pallas_call x1, Pallas kernels, body(): pl.pallas_call(functools.partial(kernel, segments, devices, blocks), out_...  42.5 us

profile of v7, /device:TPU:0, one launch (start us, length us, event | category | flops | bytes accessed | tf_op | source)
XLA Modules:
  0.0 44.0 jit_solution(2944136169251021559)
XLA Ops:
  0.7 42.5 %shard_map.109 = bf16[4,512,128]{2,1,0:T(8,128)(2,1)S(1)} custom-call(bf16[4,512,128]{2,1,0:T(8,128)(2,1)} %bitcast.4, bf16[49,2,128]{2,1,0:T(2,128)(2,1)} %bitcast.5, bf16[2,128]{1,0:T(2,128)(2,1)} %bias.1, bf16[2,128]{1,0:T(2,128)(2,1)} %gain.1, bf16[2,128,512]{2,1,0:T(8,128)(2,1)} %up.1, bf16[2,512]{1,0:T(2,128)(2,1)} %up_bias.1, ...), custom_call_target="tpu_custom_call" | custom-call | tf_op jit(solution)/shard_map/pallas_call | solution.py:573
  43.2 0.8 %copy.13 = bf16[1,4,8,8,8,128]{5,4,3,2,1,0:T(8,128)(2,1)} copy(bf16[1,4,8,8,8,128]{5,4,3,2,1,0:T(8,128)(2,1)S(1)} %bitcast.3) | data formatting | bytes 1048576
